TPU v7x, 32 devices: a whole 2x2x4 slice. The times are simulated.
32 devices in a mesh: slab: 8 (over y, x, core), head: 4 (over z).
Axes of the slice: x: 2, y: 2, z: 4, core: 2. Of those that a mesh axis runs over, the one named last changes fastest.
Arguments:
- section_activations: bfloat16 [224, 384, 256], P('slab'), may hold values from -6 to 6
- kernel_weight: bfloat16 [27, 384, 384], replicated, may hold values from -0.0625 to 0.0625
- packed_output_gradient: bfloat16 [128, 384, 256], P('slab', 'head'), may hold values from -6 to 6
- clip_length: int32 [16], replicated, may hold values from 1 to 27, as said below
- clip_slab_index: int32 [16], replicated, may hold values from 0 to 7, as said below
- packed_clip_order: int32 [16], replicated, may hold values from 0 to 15, each once
Outputs:
- input_grad: bfloat16 [224, 384, 256], P('slab', 'head')
- weight_grad: bfloat16 [27, 384, 384], P(None, 'slab', 'head')
Inputs may be any that keep to these rules, and one draw needn't show every extreme that they name: `clip_length`: the lengths of all clips sum to 128. `clip_slab_index`: every slab takes exactly two clips; the frames of a slab lie between 4 and 28, and in every draw one slab holds 28 frames and one holds 4. `packed_clip_order`: each clip appears once.
All inputs are finite; a program needn't handle non-finite values.
Results may differ from a plain program's by a relative error of at most 0.014.
Values may be sent and summed in bfloat16 or wider, within the bound.
No kernel may reach another device: no remote copies, remote signals or barrier semaphores. Data moves between devices by JAX's collectives and lax.ppermute only.
A program may use at most 448 MiB of HBM per device.

v0:
```python
import functools
import math

import jax
import jax.numpy as jnp
import numpy as np
from jax import lax
from jax.experimental import pallas as pl
from jax.experimental.pallas import tpu as pltpu
from jax.sharding import PartitionSpec as P

PIXEL_ROWS = 16
PIXEL_COLUMNS = 16
PIXELS = PIXEL_ROWS * PIXEL_COLUMNS
MIB = 1024 * 1024


def clip_places(clip_lengths, slabs, order):
    clip_ids = jnp.arange(clip_lengths.shape[0], dtype=jnp.int32)
    same_slab = slabs[None, :] == slabs[:, None]
    earlier = clip_ids[None, :] < clip_ids[:, None]
    encoder_offset = jnp.sum(jnp.where(same_slab & earlier, clip_lengths[None, :], 0), axis=1)
    matches = order[None, :] == clip_ids[:, None]
    placing = jnp.sum(jnp.where(matches, clip_ids[None, :], 0), axis=1)
    prior_frames = placing[None, :] < placing[:, None]
    packed_start = jnp.sum(jnp.where(prior_frames, clip_lengths[None, :], 0), axis=1)
    return encoder_offset, packed_start


def slot_lookup(clip_lengths, slabs, encoder_offset, packed_start, slab_number, slots):
    slot_list = jnp.arange(slots, dtype=jnp.int32)[:, None]
    lag = slot_list - encoder_offset[None, :]
    inside = (slabs[None, :] == slab_number) & (lag >= 0) & (lag < clip_lengths[None, :])
    age = jnp.sum(jnp.where(inside, lag + 1, 0), axis=1) - 1
    row = jnp.sum(jnp.where(inside, packed_start[None, :] + lag + 1, 0), axis=1) - 1
    return age, row


def row_ages(clip_lengths, packed_start, rows):
    lag = rows[:, None] - packed_start[None, :]
    inside = (lag >= 0) & (lag < clip_lengths[None, :])
    return jnp.sum(jnp.where(inside, lag + 1, 0), axis=1) - 1


def row_slot(clip_lengths, slabs, encoder_offset, packed_start, rows):
    lag = rows[:, None] - packed_start[None, :]
    inside = (lag >= 0) & (lag < clip_lengths[None, :])
    slab = jnp.sum(jnp.where(inside, slabs[None, :], 0), axis=1)
    slot = jnp.sum(jnp.where(inside, encoder_offset[None, :] + lag, 0), axis=1)
    return slab, slot


def tap_offsets():
    return [(1 - row_tap, 1 - col_tap) for row_tap in range(3) for col_tap in range(3)]


def tap_masks():
    row, column = np.divmod(np.arange(PIXELS), PIXEL_COLUMNS)
    masks = []
    for row_step, col_step in tap_offsets():
        good = (0 <= row + row_step) & (row + row_step < PIXEL_ROWS)
        good &= (0 <= column + col_step) & (column + col_step < PIXEL_COLUMNS)
        masks.append(np.broadcast_to(good, (16, PIXELS)))
    return jnp.asarray(np.stack(masks), jnp.bfloat16)


def pixel_taps(frame, masks):
    taps = []
    for t, (row_step, col_step) in enumerate(tap_offsets()):
        offset = row_step * PIXEL_COLUMNS + col_step
        if offset:
            moved = pltpu.roll(frame, (-offset) % PIXELS, 1).reshape(-1, 16, PIXELS)
            taps.append((moved * masks[t][None]).reshape(frame.shape))
        else:
            taps.append(frame)
    return taps


def input_kernel(heads, ages, places, masks, weight, *rest):
    pieces, (out, windows, taps, sems) = rest[:heads], rest[heads:]
    frames, group = out.shape[1:3]
    channels = heads * group
    copies = [
        pltpu.make_async_copy(pieces[k], windows.at[places[k]], sems.at[k]) for k in range(heads)
    ]
    for copy in copies:
        copy.start()
    for copy in copies:
        copy.wait()
    for r in range(frames + 2):
        for g in range(heads):
            for t, tap in enumerate(pixel_taps(windows[g, r], masks)):
                start = t * channels + g * group
                taps[r, start : start + group, :] = tap
        f = r - 2
        if f < 0:
            continue
        total = None
        for d in range(3):
            kernel = jnp.concatenate([weight[9 * (2 - d) + t] for t in range(9)], axis=1)
            term = jnp.dot(kernel, taps[f + d], preferred_element_type=jnp.float32)
            if d == 0:
                total = term
            else:
                total = total + jnp.where(ages[f + d] >= d, term, 0.0)
        for g in range(heads):
            out[g, f] = total[g * group : (g + 1) * group, :].astype(jnp.bfloat16)


def input_part(pieces, weight, ages, places, masks):
    heads = len(pieces)
    frames, group = pieces[0].shape[0] - 2, pieces[0].shape[1]
    channels = heads * group
    smem = pl.BlockSpec(memory_space=pltpu.SMEM)
    vmem = pl.BlockSpec(memory_space=pltpu.VMEM)
    anywhere = pl.BlockSpec(memory_space=pl.ANY)
    return pl.pallas_call(
        functools.partial(input_kernel, heads),
        out_shape=jax.ShapeDtypeStruct((heads, frames, group, PIXELS), jnp.bfloat16),
        in_specs=[smem, smem, vmem, vmem] + [anywhere] * heads,
        out_specs=vmem,
        scratch_shapes=[
            pltpu.VMEM((heads, frames + 2, group, PIXELS), jnp.bfloat16),
            pltpu.VMEM((frames + 2, 9 * channels, PIXELS), jnp.bfloat16),
            pltpu.SemaphoreType.DMA((heads,)),
        ],
        compiler_params=pltpu.CompilerParams(vmem_limit_bytes=32 * MIB),
        cost_estimate=pl.CostEstimate(
            flops=2 * frames * 27 * channels * channels * PIXELS,
            bytes_accessed=2 * 27 * channels * channels,
            transcendentals=0,
        ),
        name="input_grad_part",
    )(ages, places, masks, weight, *pieces)


def early_kernel(masks, weight, out):
    out[...] = masks[...]


def ask_early(masks, weight):
    vmem = pl.BlockSpec(memory_space=pltpu.VMEM)
    return pl.pallas_call(
        early_kernel,
        out_shape=jax.ShapeDtypeStruct(masks.shape, masks.dtype),
        in_specs=[vmem, vmem],
        out_specs=vmem,
        compiler_params=pltpu.CompilerParams(vmem_limit_bytes=16 * MIB),
        name="ask_early",
    )(masks, weight)


def fetch_rows(sources, rows, pieces, target, sems, start, first=0):
    def slot(j, carry):
        if start:
            for p, piece in enumerate(pieces):

                @pl.when(sources[j] == p)
                def _():
                    row = piece.at[rows[j], pl.ds(first, target.shape[1])]
                    pltpu.make_async_copy(row, target.at[j], sems.at[j]).start()

        else:

            @pl.when(sources[j] >= 0)
            def _():
                row = pieces[0].at[0, pl.ds(first, target.shape[1])]
                pltpu.make_async_copy(row, target.at[j], sems.at[j]).wait()

        return carry

    lax.fori_loop(0, target.shape[0], slot, 0)


def blank_rows(sources, target):
    def slot(j, carry):
        @pl.when(sources[j] < 0)
        def _():
            target[j] = jnp.zeros(target.shape[1:], target.dtype)

        return carry

    lax.fori_loop(0, target.shape[0], slot, 0)


def weight_kernel(chunk, scale, half, ages, sources, rows, parity, steps, masks, x, *rest):
    pieces, rest = rest[:-9], rest[-9:]
    mine, theirs, seen, grads, even, odd, total, sems, seen_sems = rest
    slots, group = grads.shape[0], grads.shape[1]
    channels = x.shape[1]
    span = 2 * chunk

    def fetch_seen(p):
        part = pl.ds(p * span, span)
        return pltpu.make_async_copy(x.at[part], seen.at[part], seen_sems.at[p])

    fetch_rows(sources, rows, pieces, grads, sems, True, half * group)
    for p in range(slots // span):
        fetch_seen(p).start()
    total[...] = jnp.zeros_like(total)
    blank_rows(sources, grads)
    fetch_rows(sources, rows, pieces, grads, sems, False, half * group)

    def build(first, taps):
        for f in range(chunk):
            frame = grads[jnp.minimum(first + f, slots - 1)]
            for t, tap in enumerate(pixel_taps(frame, masks)):
                taps[t * group : (t + 1) * group, f * PIXELS : (f + 1) * PIXELS] = tap

    def multiply(first, taps):
        parts = []
        for d in range(3):
            row = []
            for f in range(chunk):
                slot = first + f
                frame = seen[jnp.clip(slot - d, 0, slots - 1)]
                row.append(jnp.where(ages[slot] >= d, frame, jnp.zeros_like(frame)))
            parts.append(jnp.concatenate(row, axis=1))
        total[...] += lax.dot_general(
            jnp.concatenate(parts, axis=0),
            taps[...],
            (((1,), (1,)), ((), ())),
            preferred_element_type=jnp.float32,
        )

    build(0, even)

    def step(p, carry):
        first = 2 * p * chunk
        fetch_seen(p).wait()
        build(first + chunk, odd)
        multiply(first, even)
        build(first + 2 * chunk, even)
        multiply(first + chunk, odd)
        return carry

    def finish(p, carry):
        fetch_seen(p).wait()
        return carry

    lax.fori_loop(0, steps[0], step, 0)
    lax.fori_loop(steps[0], slots // span, finish, 0)
    chips, block = mine.shape[0], mine.shape[2]
    for j in range(chips):
        for target, side in ((mine, parity[0]), (theirs, 1 - parity[0])):
            start = pl.multiple_of((2 * j + side) * block, 8)
            for d in range(3):
                terms = total[pl.ds(d * channels + start, block), :] * scale
                target[j, 2 - d] = terms.astype(jnp.bfloat16)


def weight_part(half, halves, pieces, x, ages, sources, rows, parity, scale, count):
    slots, channels = x.shape[0], x.shape[1]
    group = pieces[0].shape[1] // halves
    chunk = 2
    assert slots % (2 * chunk) == 0
    filled = jnp.sum((ages >= 0).astype(jnp.int32))
    steps = ((filled + 2 * chunk - 1) // (2 * chunk)).reshape((1,))
    ages = jnp.concatenate([ages, jnp.full((2 * chunk,), -1, jnp.int32)])
    smem = pl.BlockSpec(memory_space=pltpu.SMEM)
    vmem = pl.BlockSpec(memory_space=pltpu.VMEM)
    anywhere = pl.BlockSpec(memory_space=pl.ANY)
    blocks = jax.ShapeDtypeStruct((count // 2, 3, channels // count, 9 * group), jnp.bfloat16)
    tap_buffer = pltpu.VMEM((9 * group, chunk * PIXELS), jnp.bfloat16)
    return pl.pallas_call(
        functools.partial(weight_kernel, chunk, scale, half),
        out_shape=(blocks, blocks),
        in_specs=[smem] * 5 + [vmem] + [anywhere] * (1 + len(pieces)),
        out_specs=(vmem, vmem),
        scratch_shapes=[
            pltpu.VMEM(x.shape, jnp.bfloat16),
            pltpu.VMEM((slots, group, PIXELS), jnp.bfloat16),
            tap_buffer,
            tap_buffer,
            pltpu.VMEM((3 * channels, 9 * group), jnp.float32),
            pltpu.SemaphoreType.DMA((slots,)),
            pltpu.SemaphoreType.DMA((slots // (2 * chunk),)),
        ],
        compiler_params=pltpu.CompilerParams(vmem_limit_bytes=59 * MIB),
        cost_estimate=pl.CostEstimate(
            flops=2 * slots * 27 * channels * group * PIXELS,
            bytes_accessed=2 * slots * channels * PIXELS,
            transcendentals=0,
        ),
        name="weight_grad_part",
    )(ages, sources, rows, parity, steps, tap_masks(), x, *pieces)


def pick_kernel(targets, *rest):
    pieces, (here, there, sems) = rest[:-3], rest[-3:]
    slots = here.shape[0]
    places = [(piece, r) for piece in pieces for r in range(piece.shape[0])]
    for start in (True, False):
        for i, (piece, r) in enumerate(places):
            target = targets[i]

            @pl.when((target >= 0) & (target < slots))
            def _():
                copy = pltpu.make_async_copy(piece.at[r], here.at[target], sems.at[i])
                copy.start() if start else copy.wait()

            @pl.when(target >= slots)
            def _():
                copy = pltpu.make_async_copy(piece.at[r], there.at[target - slots], sems.at[i])
                copy.start() if start else copy.wait()


def pick_rows(pieces, targets, slots):
    smem = pl.BlockSpec(memory_space=pltpu.SMEM)
    vmem = pl.BlockSpec(memory_space=pltpu.VMEM)
    anywhere = pl.BlockSpec(memory_space=pl.ANY)
    frames = jax.ShapeDtypeStruct((slots,) + pieces[0].shape[1:], jnp.bfloat16)
    return pl.pallas_call(
        pick_kernel,
        out_shape=(frames, frames),
        in_specs=[smem] + [anywhere] * len(pieces),
        out_specs=(vmem, vmem),
        scratch_shapes=[pltpu.SemaphoreType.DMA((targets.shape[0],))],
        compiler_params=pltpu.CompilerParams(vmem_limit_bytes=60 * MIB),
        cost_estimate=pl.CostEstimate(
            flops=0, bytes_accessed=16 * frames.size, transcendentals=0
        ),
        name="pick_rows",
    )(targets, *pieces)


def swap(value, axis, flip):
    return lax.ppermute(value, axis, [(i, i ^ flip) for i in range(lax.axis_size(axis))])


def to_chips(piece, count):
    flips = (2, 4) if count == 8 else range(2, count, 2)
    return [piece] + [swap(piece, "slab", k) for k in flips]


def passed_on(chips, count):
    if count != 8:
        return []
    half = chips[0].shape[0] // 2
    return [swap(chips[1][:half], "slab", 4), swap(chips[2][half:], "slab", 2)]


def piece_row(chip, row, rows, count):
    if count != 8:
        return chip, row
    half = rows // 2
    second = (chip == 3) & (row >= half)
    return chip + second.astype(jnp.int32), row - jnp.where(second, half, 0)


def joined(parts):
    shape = (len(parts),) + parts[0].shape
    place = lax.broadcasted_iota(jnp.int32, shape, 0)
    whole = jnp.broadcast_to(parts[0][None], shape)
    for k, part in enumerate(parts[1:], 1):
        whole = jnp.where(place == k, part[None], whole)
    return whole.reshape((-1,) + shape[2:])


def with_siblings(chips):
    return chips + [swap(piece, "slab", 1) for piece in chips]


def shards(
    section_activations,
    kernel_weight,
    packed_output_gradient,
    clip_length,
    clip_slab_index,
    packed_clip_order,
):
    slots, channels = section_activations.shape[:2]
    rows, group = packed_output_gradient.shape[:2]
    count, heads = lax.axis_size("slab"), lax.axis_size("head")
    me, head = lax.axis_index("slab"), lax.axis_index("head")
    each, frame = rows // heads, packed_output_gradient.shape[1:]

    after = lax.ppermute(
        packed_output_gradient[:2], "slab", [(i, (i - 1) % count) for i in range(count)]
    )
    longer = jnp.concatenate([packed_output_gradient, after], axis=0)
    windows = [
        lax.dynamic_slice_in_dim(longer, each * (head ^ k), each + 2, 0) for k in range(heads)
    ]
    piece, windows = lax.optimization_barrier((packed_output_gradient, windows))
    windows = windows[:1] + [swap(windows[k], "head", k) for k in range(1, heads)]
    gradient_chips = to_chips(piece, count)
    gradient_late = passed_on(gradient_chips, count)
    masks, windows[1] = lax.optimization_barrier((tap_masks(), windows[1]))
    masks = ask_early(masks, kernel_weight)

    encoder_offset, packed_start = clip_places(clip_length, clip_slab_index, packed_clip_order)
    parity = (me % 2).reshape((1,)).astype(jnp.int32)
    slot_age, slot_row = slot_lookup(
        clip_length, clip_slab_index, encoder_offset, packed_start, me, slots
    )
    shard, inner = jnp.maximum(slot_row, 0) // rows, jnp.maximum(slot_row, 0) % rows
    side, chip = (shard ^ me) % 2, (shard // 2) ^ (me // 2)
    source, source_row = piece_row(chip, inner, rows, count)
    source = jnp.where(slot_row >= 0, side * (5 if count == 8 else count // 2) + source, -1)
    places = head ^ jnp.arange(heads, dtype=jnp.int32)
    window_rows = rows * me + each * head + jnp.arange(each + 2, dtype=jnp.int32)
    window_age = row_ages(clip_length, packed_start, window_rows)

    shape = (count // 2, heads, each)
    chip, place, row = (lax.broadcasted_iota(jnp.int32, shape, d) for d in range(3))
    packed_row = (2 * (chip ^ (me // 2)) + me % 2) * rows + (place ^ head) * each + row
    slab, slot = row_slot(
        clip_length, clip_slab_index, encoder_offset, packed_start, packed_row.reshape(-1)
    )
    targets = jnp.where(slab == me, slot, jnp.where(slab == me ^ 1, slots + slot, -1))
    window_age, slot_age, source, source_row, targets = lax.optimization_barrier(
        (window_age, slot_age, source, source_row, targets)
    )

    parts = input_part(windows, kernel_weight, window_age, places, masks)
    parts, gradient_late = lax.optimization_barrier((parts, gradient_late))
    beside = with_siblings(gradient_chips)[len(gradient_chips) :]
    gradient_pieces = gradient_chips + gradient_late + beside
    gradient_pieces += with_siblings(gradient_late)[len(gradient_late) :]
    sent = [lax.dynamic_index_in_dim(parts, head ^ k, 0, keepdims=False) for k in range(heads)]
    arrived = sent[:1] + [swap(sent[k], "head", k) for k in range(1, heads)]

    scale = 1.0 / math.sqrt(rows * count * PIXELS)
    halves = 2 if group % 32 == 0 else 1

    def weight_half(half, x):
        return weight_part(
            half, halves, gradient_pieces, x, slot_age, source, source_row, parity, scale, count
        )

    x, sent = lax.optimization_barrier((section_activations, sent))
    mine, theirs = weight_half(0, x)
    mine, theirs, arrived = lax.optimization_barrier((mine, theirs, arrived))
    chips = to_chips(joined(arrived), count)
    mines, others = [mine], [swap(theirs, "slab", 1)]
    if halves == 2:
        x, chips[0], others = lax.optimization_barrier((x, chips[0], others))
        mine, theirs = weight_half(1, x)
        mine, chips, others = lax.optimization_barrier((mine, chips, others))
        mines.append(mine)
        others.append(swap(theirs, "slab", 1))

    chips = chips + passed_on(chips, count)

    mine, other = jnp.stack(mines, axis=1), jnp.stack(others, axis=1)
    rounded = (mine.astype(jnp.float32) + other.astype(jnp.float32)).astype(jnp.bfloat16)
    my_chip = me // 2
    weight_grad = sum(
        lax.dynamic_index_in_dim(term, my_chip, 0, keepdims=False).astype(jnp.float32)
        for term in (mine, other)
    )
    terms = []
    for k in range(1, count // 2):
        term = lax.dynamic_index_in_dim(rounded, my_chip ^ k, 0, keepdims=False)
        terms.append(swap(term, "slab", 2 * k))
    terms, chips = lax.optimization_barrier((terms, chips))
    for term in terms:
        weight_grad = weight_grad + term.astype(jnp.float32)
    block = channels // count
    weight_grad = weight_grad.astype(jnp.bfloat16).reshape(halves, 3, block, 9, group // halves)
    weight_grad = weight_grad.transpose(1, 3, 2, 0, 4).reshape(27, block, group)

    here, there = pick_rows(chips, targets, slots)
    there = swap(there, "slab", 1)
    frames = jnp.where((side == 0)[:, None, None], here, there)
    input_grad = jnp.where((slot_row >= 0)[:, None, None], frames, jnp.zeros_like(frames))
    return (input_grad, weight_grad)


def solution(mesh):
    return jax.shard_map(
        shards,
        mesh=mesh,
        in_specs=(P("slab", None, None), P(), P("slab", "head", None), P(), P(), P()),
        out_specs=(P("slab", "head", None), P(None, "slab", "head")),
        check_vma=False,
    )
```

profile of v0, /device:TPU:9, one launch (start us, length us, event | category | flops | bytes accessed | tf_op | source)
XLA Modules:
  0.0 131.3 jit_solution(2944008336332175258)
XLA Ops:
  5.8 2.1 %collective-permute-start.4 = (bf16[16,96,256]{2,1,0:T(8,128)(2,1)S(1)}, bf16[16,96,256]{2,1,0:T(8,128)(2,1)S(1)}, u32[]{:S(2)}, u32[]{:S(2)}) collective-permute-start(bf16[16,96,256]{2,1,0:T(8,128)(2,1)S(1)} %copy-done.7), channel_id=1, source_target_pairs={{0,8},{4,12},{8,0},{12,4},{16,24},{20,28},{24,16},{28,20},{1,9},{5... | collective-permute-start | bytes 2359304 | tf_op jit(solution)/shard_map/ppermute | solution.py:328
  7.9 1.2 collective-permute-start.6
  10.7 2.3 %collective-permute-start.2 = (bf16[6,96,256]{2,1,0:T(8,128)(2,1)S(1)}, bf16[6,96,256]{2,1,0:T(8,128)(2,1)S(1)}, u32[]{:S(2)}, u32[]{:S(2)}) collective-permute-start(bf16[6,96,256]{2,1,0:T(8,128)(2,1)S(1)} %get-tuple-element.55), channel_id=1, source_target_pairs={{0,2},{1,3},{2,0},{3,1},{4,6},{5,7},{6,4},{7,5},{8,10},{9,11},{10,... | collective-permute-start | bytes 884744 | tf_op jit(solution)/shard_map/ppermute | solution.py:328
  13.1 9.6 %collective-permute-done.1.rest_1_ = bf16[6,96,256]{2,1,0:T(8,128)(2,1)S(1)} collective-permute-done((bf16[6,96,256]{2,1,0:T(8,128)(2,1)S(1)}, bf16[6,96,256]{2,1,0:T(8,128)(2,1)S(1)}, u32[]{:S(2)}, u32[]{:S(2)}) %collective-permute-start.1) | collective-permute-done | bytes 294944 | tf_op jit(solution)/shard_map/ppermute | solution.py:328
  22.7 3.3 %copy-done = bf16[27,384,384]{2,1,0:T(8,128)(2,1)S(1)} copy-done((bf16[27,384,384]{2,1,0:T(8,128)(2,1)S(1)}, bf16[27,384,384]{2,1,0:T(8,128)(2,1)}, u32[]{:S(2)}) %copy-start) | copy-done | bytes 7962648
  27.1 1.7 %slice.21 = bf16[8,96,256]{2,1,0:T(8,128)(2,1)S(1)} slice(bf16[16,96,256]{2,1,0:T(8,128)(2,1)} %collective-permute-done.6.rest_2_), slice={[8:16], [0:96], [0:256]} | slice | bytes 786432 | tf_op jit(solution)/shard_map/slice | solution.py:340
  29.3 3.1 %collective-permute-done.2.rest_2_ = bf16[6,96,256]{2,1,0:T(8,128)(2,1)S(1)} collective-permute-done((bf16[6,96,256]{2,1,0:T(8,128)(2,1)S(1)}, bf16[6,96,256]{2,1,0:T(8,128)(2,1)S(1)}, u32[]{:S(2)}, u32[]{:S(2)}) %collective-permute-start.2) | collective-permute-done | bytes 294944 | tf_op jit(solution)/shard_map/ppermute | solution.py:328
  32.4 7.0 %collective-permute-done.3.rest_3_ = bf16[6,96,256]{2,1,0:T(8,128)(2,1)S(1)} collective-permute-done((bf16[6,96,256]{2,1,0:T(8,128)(2,1)S(1)}, bf16[6,96,256]{2,1,0:T(8,128)(2,1)S(1)}, u32[]{:S(2)}, u32[]{:S(2)}) %collective-permute-start.3) | collective-permute-done | bytes 294944 | tf_op jit(solution)/shard_map/ppermute | solution.py:328
  39.4 9.6 %input_grad_part.1 = bf16[4,4,96,256]{3,2,1,0:T(8,128)(2,1)S(1)} custom-call(s32[6]{0:T(128)S(1)} %broadcast_add_fusion.ages, s32[4]{0:T(128)S(1)} %iota_xor_fusion.places, bf16[9,16,256]{2,1,0:T(8,128)(2,1)S(1)} %ask_early.1.masks, bf16[27,384,384]{2,1,0:T(8,128)(2,1)S(1)} %copy-done.1, bf16[6,96,256]{2,1,0:T(8,128)(2,1)S(1)} %get-tuple-element.53.rest_0_, ...), custom_call_target="tpu_custom_call" | custom-call | flops 8153726976 | bytes 7962624 | tf_op jit(solution)/shard_map/input_grad_part/pallas_call | solution.py:117
  51.7 2.5 %collective-permute-start.14 = (bf16[4,96,256]{2,1,0:T(8,128)(2,1)S(1)}, bf16[4,96,256]{2,1,0:T(8,128)(2,1)S(1)}, u32[]{:S(2)}, u32[]{:S(2)}) collective-permute-start(bf16[4,96,256]{2,1,0:T(8,128)(2,1)S(1)} %get-tuple-element.109), channel_id=1, source_target_pairs={{0,2},{1,3},{2,0},{3,1},{4,6},{5,7},{6,4},{7,5},{8,10},{9,11},{10,... | collective-permute-start | bytes 589832 | tf_op jit(solution)/shard_map/ppermute | solution.py:328
  54.3 13.2 %weight_grad_part.2 = (bf16[4,3,48,432]{3,2,1,0:T(8,128)(2,1)}, bf16[4,3,48,432]{3,2,1,0:T(8,128)(2,1)}) custom-call(s32[32]{0:T(128)} %concatenate.7.ages, s32[28]{0:T(128)} %add_select_fusion.sources, s32[28]{0:T(128)} %get-tuple-element.49.rows, s32[1]{0:T(128)} %bitcast.parity, s32[1]{0:T(128)} %bitcast.1.steps, ...), custom_call_target="tpu_custom_call" | custom-call | flops 7134511104 | bytes 5505024 | tf_op jit(solution)/shard_map/weight_grad_part/pallas_call | solution.py:265
  67.5 3.8 %collective-permute-done.15 = bf16[4,96,256]{2,1,0:T(8,128)(2,1)S(1)} collective-permute-done((bf16[4,96,256]{2,1,0:T(8,128)(2,1)S(1)}, bf16[4,96,256]{2,1,0:T(8,128)(2,1)S(1)}, u32[]{:S(2)}, u32[]{:S(2)}) %collective-permute-start.15) | collective-permute-done | bytes 196640 | tf_op jit(solution)/shard_map/ppermute | solution.py:328
  71.3 1.5 %collective-permute-start.16 = (bf16[4,3,48,432]{3,2,1,0:T(8,128)(2,1)}, bf16[4,3,48,432]{3,2,1,0:T(8,128)(2,1)S(1)}, u32[]{:S(2)}, u32[]{:S(2)}) collective-permute-start(bf16[4,3,48,432]{3,2,1,0:T(8,128)(2,1)} %get-tuple-element.69), channel_id=1, source_target_pairs={{0,4},{4,0},{8,12},{12,8},{16,20},{20,16},{24,28},{28,24},{1,5},{5... | collective-permute-start | bytes 1493000 | tf_op jit(solution)/shard_map/ppermute | solution.py:328
  74.7 13.3 %weight_grad_part.3 = (bf16[4,3,48,432]{3,2,1,0:T(8,128)(2,1)}, bf16[4,3,48,432]{3,2,1,0:T(8,128)(2,1)}) custom-call(s32[32]{0:T(128)} %concatenate.7.ages, s32[28]{0:T(128)} %add_select_fusion.sources, s32[28]{0:T(128)} %get-tuple-element.49.rows, s32[1]{0:T(128)} %bitcast.parity, s32[1]{0:T(128)} %bitcast.1.steps, ...), custom_call_target="tpu_custom_call" | custom-call | flops 7134511104 | bytes 5505024 | tf_op jit(solution)/shard_map/weight_grad_part/pallas_call | solution.py:265
  88.1 4.9 %collective-permute-done.17.rest_1_ = bf16[16,96,256]{2,1,0:T(8,128)(2,1)} collective-permute-done((bf16[16,96,256]{2,1,0:T(8,128)(2,1)S(1)}, bf16[16,96,256]{2,1,0:T(8,128)(2,1)}, u32[]{:S(2)}, u32[]{:S(2)}) %collective-permute-start.17) | collective-permute-done | bytes 786464 | tf_op jit(solution)/shard_map/ppermute | solution.py:328
  96.0 1.2 collective-permute-start.24
  99.1 1.3 %collective-permute-start.22 = (bf16[2,3,48,432]{3,2,1,0:T(8,128)(2,1)S(1)}, bf16[2,3,48,432]{3,2,1,0:T(8,128)(2,1)}, u32[]{:S(2)}, u32[]{:S(2)}) collective-permute-start(bf16[2,3,48,432]{3,2,1,0:T(8,128)(2,1)S(1)} %get-tuple-element.101), channel_id=1, source_target_pairs={{0,24},{4,28},{8,16},{12,20},{16,8},{20,12},{24,0},{28,4},{1,25},{... | collective-permute-start | bytes 746504 | tf_op jit(solution)/shard_map/ppermute | solution.py:328
  100.4 3.6 %collective-permute-done.23.rest_3_ = bf16[8,96,256]{2,1,0:T(8,128)(2,1)S(1)} collective-permute-done((bf16[8,96,256]{2,1,0:T(8,128)(2,1)S(1)}, bf16[8,96,256]{2,1,0:T(8,128)(2,1)S(1)}, u32[]{:S(2)}, u32[]{:S(2)}) %collective-permute-start.23) | collective-permute-done | bytes 393248 | tf_op jit(solution)/shard_map/ppermute | solution.py:328
  104.0 1.5 %collective-permute-done.24.rest_4_ = bf16[8,96,256]{2,1,0:T(8,128)(2,1)S(1)} collective-permute-done((bf16[8,96,256]{2,1,0:T(8,128)(2,1)S(1)}, bf16[8,96,256]{2,1,0:T(8,128)(2,1)S(1)}, u32[]{:S(2)}, u32[]{:S(2)}) %collective-permute-start.24) | collective-permute-done | bytes 393248 | tf_op jit(solution)/shard_map/ppermute | solution.py:328
  105.5 6.3 %collective-permute-done.20 = bf16[2,3,48,432]{3,2,1,0:T(8,128)(2,1)S(1)} collective-permute-done((bf16[2,3,48,432]{3,2,1,0:T(8,128)(2,1)S(1)}, bf16[2,3,48,432]{3,2,1,0:T(8,128)(2,1)S(1)}, u32[]{:S(2)}, u32[]{:S(2)}) %collective-permute-start.20) | collective-permute-done | bytes 248864 | tf_op jit(solution)/shard_map/ppermute | solution.py:328
  112.6 6.2 %collective-permute-done.22 = bf16[2,3,48,432]{3,2,1,0:T(8,128)(2,1)} collective-permute-done((bf16[2,3,48,432]{3,2,1,0:T(8,128)(2,1)S(1)}, bf16[2,3,48,432]{3,2,1,0:T(8,128)(2,1)}, u32[]{:S(2)}, u32[]{:S(2)}) %collective-permute-start.22) | collective-permute-done | bytes 248864 | tf_op jit(solution)/shard_map/ppermute | solution.py:328
  118.8 4.2 %pick_rows.1 = (bf16[28,96,256]{2,1,0:T(8,128)(2,1)}, bf16[28,96,256]{2,1,0:T(8,128)(2,1)}) custom-call(s32[64]{0:T(128)} %compare_select_fusion.3.targets, bf16[16,96,256]{2,1,0:T(8,128)(2,1)} %copy-done.3, bf16[16,96,256]{2,1,0:T(8,128)(2,1)} %collective-permute-done.17.rest_1_, bf16[16,96,256]{2,1,0:T(8,128)(2,1)} %collective-permute-done.18.rest_2_, ...), custom_call_target="tpu_custom_call" | custom-call | bytes 11010048 | tf_op jit(solution)/shard_map/pick_rows/pallas_call | solution.py:313
  123.0 2.4 %collective-permute-start.25 = (bf16[28,96,256]{2,1,0:T(8,128)(2,1)}, bf16[28,96,256]{2,1,0:T(8,128)(2,1)}, u32[]{:S(2)}, u32[]{:S(2)}) collective-permute-start(bf16[28,96,256]{2,1,0:T(8,128)(2,1)} %get-tuple-element.86), channel_id=1, source_target_pairs={{0,4},{4,0},{8,12},{12,8},{16,20},{20,16},{24,28},{28,24},{1,5},{5... | collective-permute-start | bytes 4128776 | tf_op jit(solution)/shard_map/ppermute | solution.py:328
  128.5 2.8 %select_select_fusion = bf16[28,96,256]{2,1,0:T(8,128)(2,1)} fusion(bf16[28,96,256]{2,1,0:T(8,128)(2,1)S(1)} %copy-done.6, bf16[28,96,256]{2,1,0:T(8,128)(2,1)} %collective-permute-done.25, pred[28]{0:T(512)(128)(4,1)S(1)} %get-tuple-element.96, pred[28]{0:T(512)(128)(4,1)S(1)} %get-tuple-element.112), kind=kLoop, calls=%fused_computation.1 | loop fusion | flops 1376256 | bytes 4128824 | tf_op jit(solution)/shard_map/jit(_where)/select_n | solution.py:467
  (111 shorter events, 21.0 us)
Async XLA Ops:
  1.6 4.1 %collective-permute-start = (bf16[2,96,256]{2,1,0:T(8,128)(2,1)S(1)}, bf16[2,96,256]{2,1,0:T(8,128)(2,1)S(1)}, u32[]{:S(2)}, u32[]{:S(2)}) collective-permute-start(bf16[2,96,256]{2,1,0:T(8,128)(2,1)S(1)} %slice.15), channel_id=1, source_target_pairs={{0,28},{4,0},{8,4},{12,8},{16,12},{20,16},{24,20},{28,24},{1,29},{... | collective-permute-start | bytes 294920 | tf_op jit(solution)/shard_map/ppermute | solution.py:378
  5.8 20.2 %collective-permute-start.4 = (bf16[16,96,256]{2,1,0:T(8,128)(2,1)S(1)}, bf16[16,96,256]{2,1,0:T(8,128)(2,1)S(1)}, u32[]{:S(2)}, u32[]{:S(2)}) collective-permute-start(bf16[16,96,256]{2,1,0:T(8,128)(2,1)S(1)} %copy-done.7), channel_id=1, source_target_pairs={{0,8},{4,12},{8,0},{12,4},{16,24},{20,28},{24,16},{28,20},{1,9},{5... | collective-permute-start | bytes 2359304 | tf_op jit(solution)/shard_map/ppermute | solution.py:328
  7.9 19.1 %collective-permute-start.6 = (bf16[16,96,256]{2,1,0:T(8,128)(2,1)S(1)}, bf16[16,96,256]{2,1,0:T(8,128)(2,1)}, u32[]{:S(2)}, u32[]{:S(2)}) collective-permute-start(bf16[16,96,256]{2,1,0:T(8,128)(2,1)S(1)} %copy-done.7), channel_id=1, source_target_pairs={{0,16},{4,20},{8,24},{12,28},{16,0},{20,4},{24,8},{28,12},{1,17},{... | collective-permute-start | bytes 2359304 | tf_op jit(solution)/shard_map/ppermute | solution.py:328
  10.5 12.2 %collective-permute-start.1 = (bf16[6,96,256]{2,1,0:T(8,128)(2,1)S(1)}, bf16[6,96,256]{2,1,0:T(8,128)(2,1)S(1)}, u32[]{:S(2)}, u32[]{:S(2)}) collective-permute-start(bf16[6,96,256]{2,1,0:T(8,128)(2,1)S(1)} %get-tuple-element.51), channel_id=1, source_target_pairs={{0,1},{1,0},{2,3},{3,2},{4,5},{5,4},{6,7},{7,6},{8,9},{9,8},{10,11... | collective-permute-start | bytes 884744 | tf_op jit(solution)/shard_map/ppermute | solution.py:328
  10.7 21.7 %collective-permute-start.2 = (bf16[6,96,256]{2,1,0:T(8,128)(2,1)S(1)}, bf16[6,96,256]{2,1,0:T(8,128)(2,1)S(1)}, u32[]{:S(2)}, u32[]{:S(2)}) collective-permute-start(bf16[6,96,256]{2,1,0:T(8,128)(2,1)S(1)} %get-tuple-element.55), channel_id=1, source_target_pairs={{0,2},{1,3},{2,0},{3,1},{4,6},{5,7},{6,4},{7,5},{8,10},{9,11},{10,... | collective-permute-start | bytes 884744 | tf_op jit(solution)/shard_map/ppermute | solution.py:328
  13.0 26.4 %collective-permute-start.3 = (bf16[6,96,256]{2,1,0:T(8,128)(2,1)S(1)}, bf16[6,96,256]{2,1,0:T(8,128)(2,1)S(1)}, u32[]{:S(2)}, u32[]{:S(2)}) collective-permute-start(bf16[6,96,256]{2,1,0:T(8,128)(2,1)S(1)} %get-tuple-element.56), channel_id=1, source_target_pairs={{0,3},{1,2},{2,1},{3,0},{4,7},{5,6},{6,5},{7,4},{8,11},{9,10},{10,... | collective-permute-start | bytes 884744 | tf_op jit(solution)/shard_map/ppermute | solution.py:328
  22.7 28.8 %collective-permute-start.8 = (bf16[16,96,256]{2,1,0:T(8,128)(2,1)S(1)}, bf16[16,96,256]{2,1,0:T(8,128)(2,1)S(1)}, u32[]{:S(2)}, u32[]{:S(2)}) collective-permute-start(bf16[16,96,256]{2,1,0:T(8,128)(2,1)S(1)} %copy-done.7), channel_id=1, source_target_pairs={{0,4},{4,0},{8,12},{12,8},{16,20},{20,16},{24,28},{28,24},{1,5},{5... | collective-permute-start | bytes 2359304 | tf_op jit(solution)/shard_map/ppermute | solution.py:328
  26.1 23.0 %collective-permute-start.5 = (bf16[8,96,256]{2,1,0:T(8,128)(2,1)S(1)}, bf16[8,96,256]{2,1,0:T(8,128)(2,1)}, u32[]{:S(2)}, u32[]{:S(2)}) collective-permute-start(bf16[8,96,256]{2,1,0:T(8,128)(2,1)S(1)} %slice.20), channel_id=1, source_target_pairs={{0,16},{4,20},{8,24},{12,28},{16,0},{20,4},{24,8},{28,12},{1,17},{... | collective-permute-start | bytes 1179656 | tf_op jit(solution)/shard_map/ppermute | solution.py:328
  28.8 20.3 %collective-permute-start.7 = (bf16[8,96,256]{2,1,0:T(8,128)(2,1)S(1)}, bf16[8,96,256]{2,1,0:T(8,128)(2,1)}, u32[]{:S(2)}, u32[]{:S(2)}) collective-permute-start(bf16[8,96,256]{2,1,0:T(8,128)(2,1)S(1)} %slice.21), channel_id=1, source_target_pairs={{0,8},{4,12},{8,0},{12,4},{16,24},{20,28},{24,16},{28,20},{1,9},{5... | collective-permute-start | bytes 1179656 | tf_op jit(solution)/shard_map/ppermute | solution.py:328
  32.4 21.9 %collective-permute-start.10 = (bf16[16,96,256]{2,1,0:T(8,128)(2,1)}, bf16[16,96,256]{2,1,0:T(8,128)(2,1)}, u32[]{:S(2)}, u32[]{:S(2)}) collective-permute-start(bf16[16,96,256]{2,1,0:T(8,128)(2,1)} %collective-permute-done.6.rest_2_), channel_id=1, source_target_pairs={{0,4},{4,0},{8,12},{12,8},{16,20},{20,16},{24,28},{28,24},{1,5},{5... | collective-permute-start | bytes 2359304 | tf_op jit(solution)/shard_map/ppermute | solution.py:328
  39.4 14.9 %collective-permute-start.9 = (bf16[16,96,256]{2,1,0:T(8,128)(2,1)S(1)}, bf16[16,96,256]{2,1,0:T(8,128)(2,1)}, u32[]{:S(2)}, u32[]{:S(2)}) collective-permute-start(bf16[16,96,256]{2,1,0:T(8,128)(2,1)S(1)} %collective-permute-done.4.rest_1_), channel_id=1, source_target_pairs={{0,4},{4,0},{8,12},{12,8},{16,20},{20,16},{24,28},{28,24},{1,5},{5... | collective-permute-start | bytes 2359304 | tf_op jit(solution)/shard_map/ppermute | solution.py:328
  49.6 4.5 %collective-permute-start.12 = (bf16[8,96,256]{2,1,0:T(8,128)(2,1)}, bf16[8,96,256]{2,1,0:T(8,128)(2,1)}, u32[]{:S(2)}, u32[]{:S(2)}) collective-permute-start(bf16[8,96,256]{2,1,0:T(8,128)(2,1)} %collective-permute-done.7.rest_4_), channel_id=1, source_target_pairs={{0,4},{4,0},{8,12},{12,8},{16,20},{20,16},{24,28},{28,24},{1,5},{5... | collective-permute-start | bytes 1179656 | tf_op jit(solution)/shard_map/ppermute | solution.py:328
  51.6 15.9 %collective-permute-start.13 = (bf16[4,96,256]{2,1,0:T(8,128)(2,1)S(1)}, bf16[4,96,256]{2,1,0:T(8,128)(2,1)S(1)}, u32[]{:S(2)}, u32[]{:S(2)}) collective-permute-start(bf16[4,96,256]{2,1,0:T(8,128)(2,1)S(1)} %get-tuple-element.110), channel_id=1, source_target_pairs={{0,1},{1,0},{2,3},{3,2},{4,5},{5,4},{6,7},{7,6},{8,9},{9,8},{10,11... | collective-permute-start | bytes 589832 | tf_op jit(solution)/shard_map/ppermute | solution.py:328
  51.7 15.8 %collective-permute-start.14 = (bf16[4,96,256]{2,1,0:T(8,128)(2,1)S(1)}, bf16[4,96,256]{2,1,0:T(8,128)(2,1)S(1)}, u32[]{:S(2)}, u32[]{:S(2)}) collective-permute-start(bf16[4,96,256]{2,1,0:T(8,128)(2,1)S(1)} %get-tuple-element.109), channel_id=1, source_target_pairs={{0,2},{1,3},{2,0},{3,1},{4,6},{5,7},{6,4},{7,5},{8,10},{9,11},{10,... | collective-permute-start | bytes 589832 | tf_op jit(solution)/shard_map/ppermute | solution.py:328
  54.1 17.2 %collective-permute-start.15 = (bf16[4,96,256]{2,1,0:T(8,128)(2,1)S(1)}, bf16[4,96,256]{2,1,0:T(8,128)(2,1)S(1)}, u32[]{:S(2)}, u32[]{:S(2)}) collective-permute-start(bf16[4,96,256]{2,1,0:T(8,128)(2,1)S(1)} %get-tuple-element.108), channel_id=1, source_target_pairs={{0,3},{1,2},{2,1},{3,0},{4,7},{5,6},{6,5},{7,4},{8,11},{9,10},{10,... | collective-permute-start | bytes 589832 | tf_op jit(solution)/shard_map/ppermute | solution.py:328
  73.7 19.3 %collective-permute-start.17 = (bf16[16,96,256]{2,1,0:T(8,128)(2,1)S(1)}, bf16[16,96,256]{2,1,0:T(8,128)(2,1)}, u32[]{:S(2)}, u32[]{:S(2)}) collective-permute-start(bf16[16,96,256]{2,1,0:T(8,128)(2,1)S(1)} %fusion.1.rest_0_), channel_id=1, source_target_pairs={{0,8},{4,12},{8,0},{12,4},{16,24},{20,28},{24,16},{28,20},{1,9},{5... | collective-permute-start | bytes 2359304 | tf_op jit(solution)/shard_map/ppermute | solution.py:328
  74.5 19.0 %collective-permute-start.18 = (bf16[16,96,256]{2,1,0:T(8,128)(2,1)S(1)}, bf16[16,96,256]{2,1,0:T(8,128)(2,1)}, u32[]{:S(2)}, u32[]{:S(2)}) collective-permute-start(bf16[16,96,256]{2,1,0:T(8,128)(2,1)S(1)} %fusion.1.rest_0_), channel_id=1, source_target_pairs={{0,16},{4,20},{8,24},{12,28},{16,0},{20,4},{24,8},{28,12},{1,17},{... | collective-permute-start | bytes 2359304 | tf_op jit(solution)/shard_map/ppermute | solution.py:328
  88.0 9.2 %collective-permute-start.19 = (bf16[4,3,48,432]{3,2,1,0:T(8,128)(2,1)}, bf16[4,3,48,432]{3,2,1,0:T(8,128)(2,1)S(1)}, u32[]{:S(2)}, u32[]{:S(2)}) collective-permute-start(bf16[4,3,48,432]{3,2,1,0:T(8,128)(2,1)} %get-tuple-element.76), channel_id=1, source_target_pairs={{0,4},{4,0},{8,12},{12,8},{16,20},{20,16},{24,28},{28,24},{1,5},{5... | collective-permute-start | bytes 1493000 | tf_op jit(solution)/shard_map/ppermute | solution.py:328
  94.5 9.6 %collective-permute-start.23 = (bf16[8,96,256]{2,1,0:T(8,128)(2,1)S(1)}, bf16[8,96,256]{2,1,0:T(8,128)(2,1)S(1)}, u32[]{:S(2)}, u32[]{:S(2)}) collective-permute-start(bf16[8,96,256]{2,1,0:T(8,128)(2,1)S(1)} %slice.18), channel_id=1, source_target_pairs={{0,16},{4,20},{8,24},{12,28},{16,0},{20,4},{24,8},{28,12},{1,17},{... | collective-permute-start | bytes 1179656 | tf_op jit(solution)/shard_map/ppermute | solution.py:328
  96.0 9.5 %collective-permute-start.24 = (bf16[8,96,256]{2,1,0:T(8,128)(2,1)S(1)}, bf16[8,96,256]{2,1,0:T(8,128)(2,1)S(1)}, u32[]{:S(2)}, u32[]{:S(2)}) collective-permute-start(bf16[8,96,256]{2,1,0:T(8,128)(2,1)S(1)} %slice.19), channel_id=1, source_target_pairs={{0,8},{4,12},{8,0},{12,4},{16,24},{20,28},{24,16},{28,20},{1,9},{5... | collective-permute-start | bytes 1179656 | tf_op jit(solution)/shard_map/ppermute | solution.py:328
  97.7 14.1 %collective-permute-start.20 = (bf16[2,3,48,432]{3,2,1,0:T(8,128)(2,1)S(1)}, bf16[2,3,48,432]{3,2,1,0:T(8,128)(2,1)S(1)}, u32[]{:S(2)}, u32[]{:S(2)}) collective-permute-start(bf16[2,3,48,432]{3,2,1,0:T(8,128)(2,1)S(1)} %get-tuple-element.103), channel_id=1, source_target_pairs={{0,8},{4,12},{8,0},{12,4},{16,24},{20,28},{24,16},{28,20},{1,9},{5... | collective-permute-start | bytes 746504 | tf_op jit(solution)/shard_map/ppermute | solution.py:328
  98.1 13.7 %collective-permute-start.21 = (bf16[2,3,48,432]{3,2,1,0:T(8,128)(2,1)S(1)}, bf16[2,3,48,432]{3,2,1,0:T(8,128)(2,1)S(1)}, u32[]{:S(2)}, u32[]{:S(2)}) collective-permute-start(bf16[2,3,48,432]{3,2,1,0:T(8,128)(2,1)S(1)} %get-tuple-element.102), channel_id=1, source_target_pairs={{0,16},{4,20},{8,24},{12,28},{16,0},{20,4},{24,8},{28,12},{1,17},{... | collective-permute-start | bytes 746504 | tf_op jit(solution)/shard_map/ppermute | solution.py:328
  99.1 19.7 %collective-permute-start.22 = (bf16[2,3,48,432]{3,2,1,0:T(8,128)(2,1)S(1)}, bf16[2,3,48,432]{3,2,1,0:T(8,128)(2,1)}, u32[]{:S(2)}, u32[]{:S(2)}) collective-permute-start(bf16[2,3,48,432]{3,2,1,0:T(8,128)(2,1)S(1)} %get-tuple-element.101), channel_id=1, source_target_pairs={{0,24},{4,28},{8,16},{12,20},{16,8},{20,12},{24,0},{28,4},{1,25},{... | collective-permute-start | bytes 746504 | tf_op jit(solution)/shard_map/ppermute | solution.py:328
  123.0 5.5 %collective-permute-start.25 = (bf16[28,96,256]{2,1,0:T(8,128)(2,1)}, bf16[28,96,256]{2,1,0:T(8,128)(2,1)}, u32[]{:S(2)}, u32[]{:S(2)}) collective-permute-start(bf16[28,96,256]{2,1,0:T(8,128)(2,1)} %get-tuple-element.86), channel_id=1, source_target_pairs={{0,4},{4,0},{8,12},{12,8},{16,20},{20,16},{24,28},{28,24},{1,5},{5... | collective-permute-start | bytes 4128776 | tf_op jit(solution)/shard_map/ppermute | solution.py:328
  (19 other events, 149.1 us)
where the time goes:
time: 132 us; the launch traced here: 131 us
  waiting for transfers between devices  47.3 us (36%)
  Pallas kernels  40.3 us (31%)
  starting transfers between devices  21 us (16%)
  local copies, waits for them, and re-layouts  13.3 us (10%)
  other arithmetic  7.76 us (6%)
  between operations  1.65 us (1%)
    ppermute x25, waiting for transfers between devices, swap(): lax.ppermute(value, axis, [(i, i ^ flip) for i in range(lax.axis_size(axi...  46.5 us
    pallas_call x2, Pallas kernels, weight_part(): pl.pallas_call(functools.partial(weight_kernel, chunk, scale, half), out_...  26.4 us
    ppermute x25, starting transfers between devices, swap(): lax.ppermute(value, axis, [(i, i ^ flip) for i in range(lax.axis_size(axi...  20.3 us
    pallas_call x1, Pallas kernels, input_part(): pl.pallas_call(functools.partial(input_kernel, heads), out_shape=jax.Shap...  9.61 us
    unnamed x35, local copies, waits for them, and re-layouts  5.23 us
    pallas_call x1, Pallas kernels, pick_rows(): pl.pallas_call(pick_kernel, out_shape=(frames, frames), in_specs=[smem] +...  4.21 us
    slice x4, local copies, waits for them, and re-layouts, passed_on(): return [swap(chips[1][:half], 'slab', 4), swap(chips[2][half:], 'slab', 2)]  3.81 us
    select_n x1, other arithmetic, shards(): jnp.where((slot_row >= 0)[:, None, None], frames, jnp.zeros_like(frames))  2.77 us
  transfers between devices with their start and end apart: 26, of which 11 were waited for; matrix products, arithmetic and copies ran while one was open for 10% of the time, Pallas kernels for 27%

commit v1 on v0

--- a/solution.py
+++ b/solution.py
@@ -150,31 +150,34 @@
     )(masks, weight)
 
 
-def fetch_rows(sources, rows, pieces, target, sems, start, first=0):
+def start_rows(targets, pieces, out, sems, first):
+    index = 0
+    for piece in pieces:
+        for r in range(piece.shape[0]):
+            target = targets[index]
+            index += 1
+
+            @pl.when(target >= 0)
+            def _():
+                row = piece.at[r, pl.ds(first, out.shape[1])]
+                pltpu.make_async_copy(row, out.at[target], sems.at[target]).start()
+
+
+def wait_rows(ages, pieces, out, sems, first):
     def slot(j, carry):
-        if start:
-            for p, piece in enumerate(pieces):
-
-                @pl.when(sources[j] == p)
-                def _():
-                    row = piece.at[rows[j], pl.ds(first, target.shape[1])]
-                    pltpu.make_async_copy(row, target.at[j], sems.at[j]).start()
-
-        else:
-
-            @pl.when(sources[j] >= 0)
-            def _():
-                row = pieces[0].at[0, pl.ds(first, target.shape[1])]
-                pltpu.make_async_copy(row, target.at[j], sems.at[j]).wait()
+        @pl.when(ages[j] >= 0)
+        def _():
+            row = pieces[0].at[0, pl.ds(first, out.shape[1])]
+            pltpu.make_async_copy(row, out.at[j], sems.at[j]).wait()
 
         return carry
 
-    lax.fori_loop(0, target.shape[0], slot, 0)
-
-
-def blank_rows(sources, target):
+    lax.fori_loop(0, out.shape[0], slot, 0)
+
+
+def blank_rows(ages, target):
     def slot(j, carry):
-        @pl.when(sources[j] < 0)
+        @pl.when(ages[j] < 0)
         def _():
             target[j] = jnp.zeros(target.shape[1:], target.dtype)
 
@@ -183,7 +186,7 @@
     lax.fori_loop(0, target.shape[0], slot, 0)
 
 
-def weight_kernel(chunk, scale, half, ages, sources, rows, parity, steps, masks, x, *rest):
+def weight_kernel(chunk, scale, half, ages, targets, parity, steps, masks, x, *rest):
     pieces, rest = rest[:-9], rest[-9:]
     mine, theirs, seen, grads, even, odd, total, sems, seen_sems = rest
     slots, group = grads.shape[0], grads.shape[1]
@@ -194,12 +197,12 @@
         part = pl.ds(p * span, span)
         return pltpu.make_async_copy(x.at[part], seen.at[part], seen_sems.at[p])
 
-    fetch_rows(sources, rows, pieces, grads, sems, True, half * group)
     for p in range(slots // span):
         fetch_seen(p).start()
+    start_rows(targets, pieces, grads, sems, half * group)
     total[...] = jnp.zeros_like(total)
-    blank_rows(sources, grads)
-    fetch_rows(sources, rows, pieces, grads, sems, False, half * group)
+    blank_rows(ages, grads)
+    wait_rows(ages, pieces, grads, sems, half * group)
 
     def build(first, taps):
         for f in range(chunk):
@@ -249,7 +252,7 @@
                 target[j, 2 - d] = terms.astype(jnp.bfloat16)
 
 
-def weight_part(half, halves, pieces, x, ages, sources, rows, parity, scale, count):
+def weight_part(half, halves, pieces, x, ages, targets, parity, scale, count):
     slots, channels = x.shape[0], x.shape[1]
     group = pieces[0].shape[1] // halves
     chunk = 2
@@ -265,7 +268,7 @@
     return pl.pallas_call(
         functools.partial(weight_kernel, chunk, scale, half),
         out_shape=(blocks, blocks),
-        in_specs=[smem] * 5 + [vmem] + [anywhere] * (1 + len(pieces)),
+        in_specs=[smem] * 4 + [vmem] + [anywhere] * (1 + len(pieces)),
         out_specs=(vmem, vmem),
         scratch_shapes=[
             pltpu.VMEM(x.shape, jnp.bfloat16),
@@ -283,7 +286,7 @@
             transcendentals=0,
         ),
         name="weight_grad_part",
-    )(ages, sources, rows, parity, steps, tap_masks(), x, *pieces)
+    )(ages, targets, parity, steps, tap_masks(), x, *pieces)
 
 
 def pick_kernel(targets, *rest):
@@ -340,14 +343,6 @@
     return [swap(chips[1][:half], "slab", 4), swap(chips[2][half:], "slab", 2)]
 
 
-def piece_row(chip, row, rows, count):
-    if count != 8:
-        return chip, row
-    half = rows // 2
-    second = (chip == 3) & (row >= half)
-    return chip + second.astype(jnp.int32), row - jnp.where(second, half, 0)
-
-
 def joined(parts):
     shape = (len(parts),) + parts[0].shape
     place = lax.broadcasted_iota(jnp.int32, shape, 0)
@@ -396,8 +391,6 @@
     )
     shard, inner = jnp.maximum(slot_row, 0) // rows, jnp.maximum(slot_row, 0) % rows
     side, chip = (shard ^ me) % 2, (shard // 2) ^ (me // 2)
-    source, source_row = piece_row(chip, inner, rows, count)
-    source = jnp.where(slot_row >= 0, side * (5 if count == 8 else count // 2) + source, -1)
     places = head ^ jnp.arange(heads, dtype=jnp.int32)
     window_rows = rows * me + each * head + jnp.arange(each + 2, dtype=jnp.int32)
     window_age = row_ages(clip_length, packed_start, window_rows)
@@ -409,8 +402,15 @@
         clip_length, clip_slab_index, encoder_offset, packed_start, packed_row.reshape(-1)
     )
     targets = jnp.where(slab == me, slot, jnp.where(slab == me ^ 1, slots + slot, -1))
-    window_age, slot_age, source, source_row, targets = lax.optimization_barrier(
-        (window_age, slot_age, source, source_row, targets)
+    shape = (2, count // 2, rows)
+    beside, chip, row = (lax.broadcasted_iota(jnp.int32, shape, d) for d in range(3))
+    packed_row = (2 * (chip ^ (me // 2)) + (beside ^ (me % 2))) * rows + row
+    slab, slot = row_slot(
+        clip_length, clip_slab_index, encoder_offset, packed_start, packed_row.reshape(-1)
+    )
+    gradient_targets = jnp.where(slab == me, slot, -1)
+    window_age, slot_age, targets, gradient_targets = lax.optimization_barrier(
+        (window_age, slot_age, targets, gradient_targets)
     )
 
     parts = input_part(windows, kernel_weight, window_age, places, masks)
@@ -426,7 +426,7 @@
 
     def weight_half(half, x):
         return weight_part(
-            half, halves, gradient_pieces, x, slot_age, source, source_row, parity, scale, count
+            half, halves, gradient_pieces, x, slot_age, gradient_targets, parity, scale, count
         )
 
     x, sent = lax.optimization_barrier((section_activations, sent))

time: 132 us -> 132 us (level)
  Pallas kernels: 40.3 us -> 24.9 us
  starting transfers between devices: 21 us -> 28.3 us
  waiting for transfers between devices: 47.3 us -> 54.3 us
    pallas_call x2, Pallas kernels: 26.4 us -> 10.9 us  [weight_part(): pl.pallas_call(functools.partial(weight_kernel, chunk, scale, half), out_...]
    ppermute x25, starting transfers between devices: 20.3 us -> 27.6 us  [swap(): lax.ppermute(value, axis, [(i, i ^ flip) for i in range(lax.axis_size(axi...]
    ppermute x25, waiting for transfers between devices: 46.5 us -> 53.3 us  [swap(): lax.ppermute(value, axis, [(i, i ^ flip) for i in range(lax.axis_size(axi...]
  transfers between devices with their start and end apart: 26 -> 26, of which waited for: 11 -> 12; matrix products, arithmetic and copies ran while one was open for 10% -> 10% of each run, Pallas kernels for 27% -> 16%
where the time goes in v1:
time: 132 us; the launch traced here: 131 us
  waiting for transfers between devices  54.3 us (41%)
  starting transfers between devices  28.3 us (21%)
  Pallas kernels  24.9 us (19%)
  local copies, waits for them, and re-layouts  14.6 us (11%)
  other arithmetic  7.34 us (6%)
  between operations  1.73 us (1%)
    ppermute x25, waiting for transfers between devices, swap(): lax.ppermute(value, axis, [(i, i ^ flip) for i in range(lax.axis_size(axi...  53.3 us
    ppermute x25, starting transfers between devices, swap(): lax.ppermute(value, axis, [(i, i ^ flip) for i in range(lax.axis_size(axi...  27.6 us
    pallas_call x2, Pallas kernels, weight_part(): pl.pallas_call(functools.partial(weight_kernel, chunk, scale, half), out_...  10.9 us
    pallas_call x1, Pallas kernels, input_part(): pl.pallas_call(functools.partial(input_kernel, heads), out_shape=jax.Shap...  9.81 us
    unnamed x35, local copies, waits for them, and re-layouts  6.09 us
    slice x4, local copies, waits for them, and re-layouts, passed_on(): return [swap(chips[1][:half], 'slab', 4), swap(chips[2][half:], 'slab', 2)]  4.24 us
    pallas_call x1, Pallas kernels, pick_rows(): pl.pallas_call(pick_kernel, out_shape=(frames, frames), in_specs=[smem] +...  4.12 us
    select_n x1, other arithmetic, shards(): jnp.where((slot_row >= 0)[:, None, None], frames, jnp.zeros_like(frames))  2.76 us
  transfers between devices with their start and end apart: 26, of which 12 were waited for; matrix products, arithmetic and copies ran while one was open for 10% of the time, Pallas kernels for 16%

profile of v1, /device:TPU:9, one launch (start us, length us, event | category | flops | bytes accessed | tf_op | source)
XLA Modules:
  0.0 131.2 jit_solution(13200131498809655973)
XLA Ops:
  5.8 2.1 %collective-permute-start.4 = (bf16[16,96,256]{2,1,0:T(8,128)(2,1)S(1)}, bf16[16,96,256]{2,1,0:T(8,128)(2,1)}, u32[]{:S(2)}, u32[]{:S(2)}) collective-permute-start(bf16[16,96,256]{2,1,0:T(8,128)(2,1)S(1)} %copy-done.7), channel_id=1, source_target_pairs={{0,8},{4,12},{8,0},{12,4},{16,24},{20,28},{24,16},{28,20},{1,9},{5... | collective-permute-start | bytes 2359304 | tf_op jit(solution)/shard_map/ppermute | solution.py:331
  7.9 1.2 collective-permute-start.6
  10.4 2.3 %collective-permute-start.2 = (bf16[6,96,256]{2,1,0:T(8,128)(2,1)S(1)}, bf16[6,96,256]{2,1,0:T(8,128)(2,1)S(1)}, u32[]{:S(2)}, u32[]{:S(2)}) collective-permute-start(bf16[6,96,256]{2,1,0:T(8,128)(2,1)S(1)} %get-tuple-element.53), channel_id=1, source_target_pairs={{0,2},{1,3},{2,0},{3,1},{4,6},{5,7},{6,4},{7,5},{8,10},{9,11},{10,... | collective-permute-start | bytes 884744 | tf_op jit(solution)/shard_map/ppermute | solution.py:331
  12.9 9.4 %collective-permute-done.1.rest_1_ = bf16[6,96,256]{2,1,0:T(8,128)(2,1)S(1)} collective-permute-done((bf16[6,96,256]{2,1,0:T(8,128)(2,1)S(1)}, bf16[6,96,256]{2,1,0:T(8,128)(2,1)S(1)}, u32[]{:S(2)}, u32[]{:S(2)}) %collective-permute-start.1) | collective-permute-done | bytes 294944 | tf_op jit(solution)/shard_map/ppermute | solution.py:331
  22.3 3.3 %copy-done = bf16[27,384,384]{2,1,0:T(8,128)(2,1)S(1)} copy-done((bf16[27,384,384]{2,1,0:T(8,128)(2,1)S(1)}, bf16[27,384,384]{2,1,0:T(8,128)(2,1)}, u32[]{:S(2)}) %copy-start) | copy-done | bytes 7962648
  26.8 1.2 collective-permute-start.5
  29.1 1.3 %collective-permute-start.7 = (bf16[8,96,256]{2,1,0:T(8,128)(2,1)S(1)}, bf16[8,96,256]{2,1,0:T(8,128)(2,1)}, u32[]{:S(2)}, u32[]{:S(2)}) collective-permute-start(bf16[8,96,256]{2,1,0:T(8,128)(2,1)S(1)} %slice.21), channel_id=1, source_target_pairs={{0,8},{4,12},{8,0},{12,4},{16,24},{20,28},{24,16},{28,20},{1,9},{5... | collective-permute-start | bytes 1179656 | tf_op jit(solution)/shard_map/ppermute | solution.py:331
  30.4 1.8 %collective-permute-done.2.rest_2_ = bf16[6,96,256]{2,1,0:T(8,128)(2,1)S(1)} collective-permute-done((bf16[6,96,256]{2,1,0:T(8,128)(2,1)S(1)}, bf16[6,96,256]{2,1,0:T(8,128)(2,1)S(1)}, u32[]{:S(2)}, u32[]{:S(2)}) %collective-permute-start.2) | collective-permute-done | bytes 294944 | tf_op jit(solution)/shard_map/ppermute | solution.py:331
  32.2 6.9 %collective-permute-done.3.rest_3_ = bf16[6,96,256]{2,1,0:T(8,128)(2,1)S(1)} collective-permute-done((bf16[6,96,256]{2,1,0:T(8,128)(2,1)S(1)}, bf16[6,96,256]{2,1,0:T(8,128)(2,1)S(1)}, u32[]{:S(2)}, u32[]{:S(2)}) %collective-permute-start.3) | collective-permute-done | bytes 294944 | tf_op jit(solution)/shard_map/ppermute | solution.py:331
  39.1 9.8 %input_grad_part.1 = bf16[4,4,96,256]{3,2,1,0:T(8,128)(2,1)S(1)} custom-call(s32[6]{0:T(128)S(1)} %broadcast_add_fusion.ages, s32[4]{0:T(128)S(1)} %iota_xor_fusion.1.places, bf16[9,16,256]{2,1,0:T(8,128)(2,1)S(1)} %ask_early.1.masks, bf16[27,384,384]{2,1,0:T(8,128)(2,1)S(1)} %copy-done.1, bf16[6,96,256]{2,1,0:T(8,128)(2,1)S(1)} %get-tuple-element.51.rest_0_, ...), custom_call_target="tpu_custom_call" | custom-call | flops 8153726976 | bytes 7962624 | tf_op jit(solution)/shard_map/input_grad_part/pallas_call | solution.py:117
  51.5 2.4 %collective-permute-start.14 = (bf16[4,96,256]{2,1,0:T(8,128)(2,1)S(1)}, bf16[4,96,256]{2,1,0:T(8,128)(2,1)S(1)}, u32[]{:S(2)}, u32[]{:S(2)}) collective-permute-start(bf16[4,96,256]{2,1,0:T(8,128)(2,1)S(1)} %get-tuple-element.104), channel_id=1, source_target_pairs={{0,2},{1,3},{2,0},{3,1},{4,6},{5,7},{6,4},{7,5},{8,10},{9,11},{10,... | collective-permute-start | bytes 589832 | tf_op jit(solution)/shard_map/ppermute | solution.py:331
  55.0 5.6 %weight_grad_part.2 = (bf16[4,3,48,432]{3,2,1,0:T(8,128)(2,1)}, bf16[4,3,48,432]{3,2,1,0:T(8,128)(2,1)}) custom-call(s32[32]{0:T(128)} %concatenate.7.ages, s32[128]{0:T(128)} %compare_select_fusion.2.targets, s32[1]{0:T(128)} %bitcast.parity, s32[1]{0:T(128)} %bitcast.1.steps, bf16[9,16,256]{2,1,0:T(8,128)(2,1)} %constant.134.clone.masks, ...), custom_call_target="tpu_custom_call" | custom-call | flops 7134511104 | bytes 5505024 | tf_op jit(solution)/shard_map/weight_grad_part/pallas_call | solution.py:268
  60.6 2.2 %collective-permute-done.14 = bf16[4,96,256]{2,1,0:T(8,128)(2,1)S(1)} collective-permute-done((bf16[4,96,256]{2,1,0:T(8,128)(2,1)S(1)}, bf16[4,96,256]{2,1,0:T(8,128)(2,1)S(1)}, u32[]{:S(2)}, u32[]{:S(2)}) %collective-permute-start.14) | collective-permute-done | bytes 196640 | tf_op jit(solution)/shard_map/ppermute | solution.py:331
  62.8 8.3 %collective-permute-done.15 = bf16[4,96,256]{2,1,0:T(8,128)(2,1)S(1)} collective-permute-done((bf16[4,96,256]{2,1,0:T(8,128)(2,1)S(1)}, bf16[4,96,256]{2,1,0:T(8,128)(2,1)S(1)}, u32[]{:S(2)}, u32[]{:S(2)}) %collective-permute-start.15) | collective-permute-done | bytes 196640 | tf_op jit(solution)/shard_map/ppermute | solution.py:331
  71.2 1.5 %collective-permute-start.16 = (bf16[4,3,48,432]{3,2,1,0:T(8,128)(2,1)}, bf16[4,3,48,432]{3,2,1,0:T(8,128)(2,1)S(1)}, u32[]{:S(2)}, u32[]{:S(2)}) collective-permute-start(bf16[4,3,48,432]{3,2,1,0:T(8,128)(2,1)} %get-tuple-element.67), channel_id=1, source_target_pairs={{0,4},{4,0},{8,12},{12,8},{16,20},{20,16},{24,28},{28,24},{1,5},{5... | collective-permute-start | bytes 1493000 | tf_op jit(solution)/shard_map/ppermute | solution.py:331
  74.7 5.4 %weight_grad_part.3 = (bf16[4,3,48,432]{3,2,1,0:T(8,128)(2,1)}, bf16[4,3,48,432]{3,2,1,0:T(8,128)(2,1)}) custom-call(s32[32]{0:T(128)} %concatenate.7.ages, s32[128]{0:T(128)} %compare_select_fusion.2.targets, s32[1]{0:T(128)} %bitcast.parity, s32[1]{0:T(128)} %bitcast.1.steps, bf16[9,16,256]{2,1,0:T(8,128)(2,1)} %constant.134.clone.masks, ...), custom_call_target="tpu_custom_call" | custom-call | flops 7134511104 | bytes 5505024 | tf_op jit(solution)/shard_map/weight_grad_part/pallas_call | solution.py:268
  80.1 6.5 %collective-permute-start.19 = (bf16[4,3,48,432]{3,2,1,0:T(8,128)(2,1)}, bf16[4,3,48,432]{3,2,1,0:T(8,128)(2,1)S(1)}, u32[]{:S(2)}, u32[]{:S(2)}) collective-permute-start(bf16[4,3,48,432]{3,2,1,0:T(8,128)(2,1)} %get-tuple-element.74), channel_id=1, source_target_pairs={{0,4},{4,0},{8,12},{12,8},{16,20},{20,16},{24,28},{28,24},{1,5},{5... | collective-permute-start | bytes 1493000 | tf_op jit(solution)/shard_map/ppermute | solution.py:331
  86.6 6.3 %collective-permute-done.17.rest_1_ = bf16[16,96,256]{2,1,0:T(8,128)(2,1)} collective-permute-done((bf16[16,96,256]{2,1,0:T(8,128)(2,1)S(1)}, bf16[16,96,256]{2,1,0:T(8,128)(2,1)}, u32[]{:S(2)}, u32[]{:S(2)}) %collective-permute-start.17) | collective-permute-done | bytes 786464 | tf_op jit(solution)/shard_map/ppermute | solution.py:331
  100.2 3.8 %collective-permute-done.23.rest_3_ = bf16[8,96,256]{2,1,0:T(8,128)(2,1)S(1)} collective-permute-done((bf16[8,96,256]{2,1,0:T(8,128)(2,1)S(1)}, bf16[8,96,256]{2,1,0:T(8,128)(2,1)S(1)}, u32[]{:S(2)}, u32[]{:S(2)}) %collective-permute-start.23) | collective-permute-done | bytes 393248 | tf_op jit(solution)/shard_map/ppermute | solution.py:331
  105.1 6.3 %collective-permute-done.20 = bf16[2,3,48,432]{3,2,1,0:T(8,128)(2,1)S(1)} collective-permute-done((bf16[2,3,48,432]{3,2,1,0:T(8,128)(2,1)S(1)}, bf16[2,3,48,432]{3,2,1,0:T(8,128)(2,1)S(1)}, u32[]{:S(2)}, u32[]{:S(2)}) %collective-permute-start.20) | collective-permute-done | bytes 248864 | tf_op jit(solution)/shard_map/ppermute | solution.py:331
  112.2 6.6 %collective-permute-done.22 = bf16[2,3,48,432]{3,2,1,0:T(8,128)(2,1)} collective-permute-done((bf16[2,3,48,432]{3,2,1,0:T(8,128)(2,1)S(1)}, bf16[2,3,48,432]{3,2,1,0:T(8,128)(2,1)}, u32[]{:S(2)}, u32[]{:S(2)}) %collective-permute-start.22) | collective-permute-done | bytes 248864 | tf_op jit(solution)/shard_map/ppermute | solution.py:331
  118.8 4.1 %pick_rows.1 = (bf16[28,96,256]{2,1,0:T(8,128)(2,1)}, bf16[28,96,256]{2,1,0:T(8,128)(2,1)}) custom-call(s32[64]{0:T(128)} %compare_select_fusion.4.targets, bf16[16,96,256]{2,1,0:T(8,128)(2,1)} %copy-done.3, bf16[16,96,256]{2,1,0:T(8,128)(2,1)} %collective-permute-done.17.rest_1_, bf16[16,96,256]{2,1,0:T(8,128)(2,1)} %collective-permute-done.18.rest_2_, ...), custom_call_target="tpu_custom_call" | custom-call | bytes 11010048 | tf_op jit(solution)/shard_map/pick_rows/pallas_call | solution.py:316
  122.9 2.3 %collective-permute-start.25 = (bf16[28,96,256]{2,1,0:T(8,128)(2,1)}, bf16[28,96,256]{2,1,0:T(8,128)(2,1)}, u32[]{:S(2)}, u32[]{:S(2)}) collective-permute-start(bf16[28,96,256]{2,1,0:T(8,128)(2,1)} %get-tuple-element.84), channel_id=1, source_target_pairs={{0,4},{4,0},{8,12},{12,8},{16,20},{20,16},{24,28},{28,24},{1,5},{5... | collective-permute-start | bytes 4128776 | tf_op jit(solution)/shard_map/ppermute | solution.py:331
  128.4 2.8 %select_select_fusion = bf16[28,96,256]{2,1,0:T(8,128)(2,1)} fusion(bf16[28,96,256]{2,1,0:T(8,128)(2,1)S(1)} %copy-done.6, bf16[28,96,256]{2,1,0:T(8,128)(2,1)} %collective-permute-done.25, pred[28]{0:T(512)(128)(4,1)S(1)} %get-tuple-element.108, pred[28]{0:T(512)(128)(4,1)S(1)} %get-tuple-element.107), kind=kLoop, calls=%fused_computation.1 | loop fusion | flops 1376256 | bytes 4128824 | tf_op jit(solution)/shard_map/jit(_where)/select_n | solution.py:467
  (116 shorter events, 26.0 us)
Async XLA Ops:
  1.6 4.1 %collective-permute-start = (bf16[2,96,256]{2,1,0:T(8,128)(2,1)S(1)}, bf16[2,96,256]{2,1,0:T(8,128)(2,1)S(1)}, u32[]{:S(2)}, u32[]{:S(2)}) collective-permute-start(bf16[2,96,256]{2,1,0:T(8,128)(2,1)S(1)} %slice.15), channel_id=1, source_target_pairs={{0,28},{4,0},{8,4},{12,8},{16,12},{20,16},{24,20},{28,24},{1,29},{... | collective-permute-start | bytes 294920 | tf_op jit(solution)/shard_map/ppermute | solution.py:373
  5.8 19.8 %collective-permute-start.4 = (bf16[16,96,256]{2,1,0:T(8,128)(2,1)S(1)}, bf16[16,96,256]{2,1,0:T(8,128)(2,1)}, u32[]{:S(2)}, u32[]{:S(2)}) collective-permute-start(bf16[16,96,256]{2,1,0:T(8,128)(2,1)S(1)} %copy-done.7), channel_id=1, source_target_pairs={{0,8},{4,12},{8,0},{12,4},{16,24},{20,28},{24,16},{28,20},{1,9},{5... | collective-permute-start | bytes 2359304 | tf_op jit(solution)/shard_map/ppermute | solution.py:331
  7.9 20.1 %collective-permute-start.6 = (bf16[16,96,256]{2,1,0:T(8,128)(2,1)S(1)}, bf16[16,96,256]{2,1,0:T(8,128)(2,1)}, u32[]{:S(2)}, u32[]{:S(2)}) collective-permute-start(bf16[16,96,256]{2,1,0:T(8,128)(2,1)S(1)} %copy-done.7), channel_id=1, source_target_pairs={{0,16},{4,20},{8,24},{12,28},{16,0},{20,4},{24,8},{28,12},{1,17},{... | collective-permute-start | bytes 2359304 | tf_op jit(solution)/shard_map/ppermute | solution.py:331
  10.3 12.1 %collective-permute-start.1 = (bf16[6,96,256]{2,1,0:T(8,128)(2,1)S(1)}, bf16[6,96,256]{2,1,0:T(8,128)(2,1)S(1)}, u32[]{:S(2)}, u32[]{:S(2)}) collective-permute-start(bf16[6,96,256]{2,1,0:T(8,128)(2,1)S(1)} %get-tuple-element.49), channel_id=1, source_target_pairs={{0,1},{1,0},{2,3},{3,2},{4,5},{5,4},{6,7},{7,6},{8,9},{9,8},{10,11... | collective-permute-start | bytes 884744 | tf_op jit(solution)/shard_map/ppermute | solution.py:331
  10.4 21.8 %collective-permute-start.2 = (bf16[6,96,256]{2,1,0:T(8,128)(2,1)S(1)}, bf16[6,96,256]{2,1,0:T(8,128)(2,1)S(1)}, u32[]{:S(2)}, u32[]{:S(2)}) collective-permute-start(bf16[6,96,256]{2,1,0:T(8,128)(2,1)S(1)} %get-tuple-element.53), channel_id=1, source_target_pairs={{0,2},{1,3},{2,0},{3,1},{4,6},{5,7},{6,4},{7,5},{8,10},{9,11},{10,... | collective-permute-start | bytes 884744 | tf_op jit(solution)/shard_map/ppermute | solution.py:331
  12.8 26.3 %collective-permute-start.3 = (bf16[6,96,256]{2,1,0:T(8,128)(2,1)S(1)}, bf16[6,96,256]{2,1,0:T(8,128)(2,1)S(1)}, u32[]{:S(2)}, u32[]{:S(2)}) collective-permute-start(bf16[6,96,256]{2,1,0:T(8,128)(2,1)S(1)} %get-tuple-element.54), channel_id=1, source_target_pairs={{0,3},{1,2},{2,1},{3,0},{4,7},{5,6},{6,5},{7,4},{8,11},{9,10},{10,... | collective-permute-start | bytes 884744 | tf_op jit(solution)/shard_map/ppermute | solution.py:331
  22.3 29.1 %collective-permute-start.8 = (bf16[16,96,256]{2,1,0:T(8,128)(2,1)S(1)}, bf16[16,96,256]{2,1,0:T(8,128)(2,1)}, u32[]{:S(2)}, u32[]{:S(2)}) collective-permute-start(bf16[16,96,256]{2,1,0:T(8,128)(2,1)S(1)} %copy-done.7), channel_id=1, source_target_pairs={{0,4},{4,0},{8,12},{12,8},{16,20},{20,16},{24,28},{28,24},{1,5},{5... | collective-permute-start | bytes 2359304 | tf_op jit(solution)/shard_map/ppermute | solution.py:331
  26.8 22.1 %collective-permute-start.5 = (bf16[8,96,256]{2,1,0:T(8,128)(2,1)S(1)}, bf16[8,96,256]{2,1,0:T(8,128)(2,1)}, u32[]{:S(2)}, u32[]{:S(2)}) collective-permute-start(bf16[8,96,256]{2,1,0:T(8,128)(2,1)S(1)} %slice.20), channel_id=1, source_target_pairs={{0,16},{4,20},{8,24},{12,28},{16,0},{20,4},{24,8},{28,12},{1,17},{... | collective-permute-start | bytes 1179656 | tf_op jit(solution)/shard_map/ppermute | solution.py:331
  29.1 19.8 %collective-permute-start.7 = (bf16[8,96,256]{2,1,0:T(8,128)(2,1)S(1)}, bf16[8,96,256]{2,1,0:T(8,128)(2,1)}, u32[]{:S(2)}, u32[]{:S(2)}) collective-permute-start(bf16[8,96,256]{2,1,0:T(8,128)(2,1)S(1)} %slice.21), channel_id=1, source_target_pairs={{0,8},{4,12},{8,0},{12,4},{16,24},{20,28},{24,16},{28,20},{1,9},{5... | collective-permute-start | bytes 1179656 | tf_op jit(solution)/shard_map/ppermute | solution.py:331
  32.2 22.0 %collective-permute-start.10 = (bf16[16,96,256]{2,1,0:T(8,128)(2,1)}, bf16[16,96,256]{2,1,0:T(8,128)(2,1)S(1)}, u32[]{:S(2)}, u32[]{:S(2)}) collective-permute-start(bf16[16,96,256]{2,1,0:T(8,128)(2,1)} %collective-permute-done.6.rest_2_), channel_id=1, source_target_pairs={{0,4},{4,0},{8,12},{12,8},{16,20},{20,16},{24,28},{28,24},{1,5},{5... | collective-permute-start | bytes 2359304 | tf_op jit(solution)/shard_map/ppermute | solution.py:331
  39.1 15.1 %collective-permute-start.9 = (bf16[16,96,256]{2,1,0:T(8,128)(2,1)}, bf16[16,96,256]{2,1,0:T(8,128)(2,1)}, u32[]{:S(2)}, u32[]{:S(2)}) collective-permute-start(bf16[16,96,256]{2,1,0:T(8,128)(2,1)} %collective-permute-done.4.rest_1_), channel_id=1, source_target_pairs={{0,4},{4,0},{8,12},{12,8},{16,20},{20,16},{24,28},{28,24},{1,5},{5... | collective-permute-start | bytes 2359304 | tf_op jit(solution)/shard_map/ppermute | solution.py:331
  49.5 4.5 %collective-permute-start.12 = (bf16[8,96,256]{2,1,0:T(8,128)(2,1)}, bf16[8,96,256]{2,1,0:T(8,128)(2,1)}, u32[]{:S(2)}, u32[]{:S(2)}) collective-permute-start(bf16[8,96,256]{2,1,0:T(8,128)(2,1)} %collective-permute-done.7.rest_4_), channel_id=1, source_target_pairs={{0,4},{4,0},{8,12},{12,8},{16,20},{20,16},{24,28},{28,24},{1,5},{5... | collective-permute-start | bytes 1179656 | tf_op jit(solution)/shard_map/ppermute | solution.py:331
  51.4 9.2 %collective-permute-start.13 = (bf16[4,96,256]{2,1,0:T(8,128)(2,1)S(1)}, bf16[4,96,256]{2,1,0:T(8,128)(2,1)S(1)}, u32[]{:S(2)}, u32[]{:S(2)}) collective-permute-start(bf16[4,96,256]{2,1,0:T(8,128)(2,1)S(1)} %get-tuple-element.105), channel_id=1, source_target_pairs={{0,1},{1,0},{2,3},{3,2},{4,5},{5,4},{6,7},{7,6},{8,9},{9,8},{10,11... | collective-permute-start | bytes 589832 | tf_op jit(solution)/shard_map/ppermute | solution.py:331
  51.5 11.3 %collective-permute-start.14 = (bf16[4,96,256]{2,1,0:T(8,128)(2,1)S(1)}, bf16[4,96,256]{2,1,0:T(8,128)(2,1)S(1)}, u32[]{:S(2)}, u32[]{:S(2)}) collective-permute-start(bf16[4,96,256]{2,1,0:T(8,128)(2,1)S(1)} %get-tuple-element.104), channel_id=1, source_target_pairs={{0,2},{1,3},{2,0},{3,1},{4,6},{5,7},{6,4},{7,5},{8,10},{9,11},{10,... | collective-permute-start | bytes 589832 | tf_op jit(solution)/shard_map/ppermute | solution.py:331
  54.0 17.2 %collective-permute-start.15 = (bf16[4,96,256]{2,1,0:T(8,128)(2,1)S(1)}, bf16[4,96,256]{2,1,0:T(8,128)(2,1)S(1)}, u32[]{:S(2)}, u32[]{:S(2)}) collective-permute-start(bf16[4,96,256]{2,1,0:T(8,128)(2,1)S(1)} %get-tuple-element.103), channel_id=1, source_target_pairs={{0,3},{1,2},{2,1},{3,0},{4,7},{5,6},{6,5},{7,4},{8,11},{9,10},{10,... | collective-permute-start | bytes 589832 | tf_op jit(solution)/shard_map/ppermute | solution.py:331
  73.6 19.3 %collective-permute-start.17 = (bf16[16,96,256]{2,1,0:T(8,128)(2,1)S(1)}, bf16[16,96,256]{2,1,0:T(8,128)(2,1)}, u32[]{:S(2)}, u32[]{:S(2)}) collective-permute-start(bf16[16,96,256]{2,1,0:T(8,128)(2,1)S(1)} %fusion.1.rest_0_), channel_id=1, source_target_pairs={{0,8},{4,12},{8,0},{12,4},{16,24},{20,28},{24,16},{28,20},{1,9},{5... | collective-permute-start | bytes 2359304 | tf_op jit(solution)/shard_map/ppermute | solution.py:331
  74.5 19.0 %collective-permute-start.18 = (bf16[16,96,256]{2,1,0:T(8,128)(2,1)S(1)}, bf16[16,96,256]{2,1,0:T(8,128)(2,1)}, u32[]{:S(2)}, u32[]{:S(2)}) collective-permute-start(bf16[16,96,256]{2,1,0:T(8,128)(2,1)S(1)} %fusion.1.rest_0_), channel_id=1, source_target_pairs={{0,16},{4,20},{8,24},{12,28},{16,0},{20,4},{24,8},{28,12},{1,17},{... | collective-permute-start | bytes 2359304 | tf_op jit(solution)/shard_map/ppermute | solution.py:331
  80.1 16.9 %collective-permute-start.19 = (bf16[4,3,48,432]{3,2,1,0:T(8,128)(2,1)}, bf16[4,3,48,432]{3,2,1,0:T(8,128)(2,1)S(1)}, u32[]{:S(2)}, u32[]{:S(2)}) collective-permute-start(bf16[4,3,48,432]{3,2,1,0:T(8,128)(2,1)} %get-tuple-element.74), channel_id=1, source_target_pairs={{0,4},{4,0},{8,12},{12,8},{16,20},{20,16},{24,28},{28,24},{1,5},{5... | collective-permute-start | bytes 1493000 | tf_op jit(solution)/shard_map/ppermute | solution.py:331
  94.5 9.6 %collective-permute-start.23 = (bf16[8,96,256]{2,1,0:T(8,128)(2,1)S(1)}, bf16[8,96,256]{2,1,0:T(8,128)(2,1)S(1)}, u32[]{:S(2)}, u32[]{:S(2)}) collective-permute-start(bf16[8,96,256]{2,1,0:T(8,128)(2,1)S(1)} %slice.18), channel_id=1, source_target_pairs={{0,16},{4,20},{8,24},{12,28},{16,0},{20,4},{24,8},{28,12},{1,17},{... | collective-permute-start | bytes 1179656 | tf_op jit(solution)/shard_map/ppermute | solution.py:331
  95.8 9.3 %collective-permute-start.24 = (bf16[8,96,256]{2,1,0:T(8,128)(2,1)S(1)}, bf16[8,96,256]{2,1,0:T(8,128)(2,1)S(1)}, u32[]{:S(2)}, u32[]{:S(2)}) collective-permute-start(bf16[8,96,256]{2,1,0:T(8,128)(2,1)S(1)} %slice.19), channel_id=1, source_target_pairs={{0,8},{4,12},{8,0},{12,4},{16,24},{20,28},{24,16},{28,20},{1,9},{5... | collective-permute-start | bytes 1179656 | tf_op jit(solution)/shard_map/ppermute | solution.py:331
  97.5 13.9 %collective-permute-start.20 = (bf16[2,3,48,432]{3,2,1,0:T(8,128)(2,1)S(1)}, bf16[2,3,48,432]{3,2,1,0:T(8,128)(2,1)S(1)}, u32[]{:S(2)}, u32[]{:S(2)}) collective-permute-start(bf16[2,3,48,432]{3,2,1,0:T(8,128)(2,1)S(1)} %get-tuple-element.98), channel_id=1, source_target_pairs={{0,8},{4,12},{8,0},{12,4},{16,24},{20,28},{24,16},{28,20},{1,9},{5... | collective-permute-start | bytes 746504 | tf_op jit(solution)/shard_map/ppermute | solution.py:331
  97.9 13.5 %collective-permute-start.21 = (bf16[2,3,48,432]{3,2,1,0:T(8,128)(2,1)S(1)}, bf16[2,3,48,432]{3,2,1,0:T(8,128)(2,1)S(1)}, u32[]{:S(2)}, u32[]{:S(2)}) collective-permute-start(bf16[2,3,48,432]{3,2,1,0:T(8,128)(2,1)S(1)} %get-tuple-element.97), channel_id=1, source_target_pairs={{0,16},{4,20},{8,24},{12,28},{16,0},{20,4},{24,8},{28,12},{1,17},{... | collective-permute-start | bytes 746504 | tf_op jit(solution)/shard_map/ppermute | solution.py:331
  99.1 19.6 %collective-permute-start.22 = (bf16[2,3,48,432]{3,2,1,0:T(8,128)(2,1)S(1)}, bf16[2,3,48,432]{3,2,1,0:T(8,128)(2,1)}, u32[]{:S(2)}, u32[]{:S(2)}) collective-permute-start(bf16[2,3,48,432]{3,2,1,0:T(8,128)(2,1)S(1)} %get-tuple-element.96), channel_id=1, source_target_pairs={{0,24},{4,28},{8,16},{12,20},{16,8},{20,12},{24,0},{28,4},{1,25},{... | collective-permute-start | bytes 746504 | tf_op jit(solution)/shard_map/ppermute | solution.py:331
  122.9 5.5 %collective-permute-start.25 = (bf16[28,96,256]{2,1,0:T(8,128)(2,1)}, bf16[28,96,256]{2,1,0:T(8,128)(2,1)}, u32[]{:S(2)}, u32[]{:S(2)}) collective-permute-start(bf16[28,96,256]{2,1,0:T(8,128)(2,1)} %get-tuple-element.84), channel_id=1, source_target_pairs={{0,4},{4,0},{8,12},{12,8},{16,20},{20,16},{24,28},{28,24},{1,5},{5... | collective-permute-start | bytes 4128776 | tf_op jit(solution)/shard_map/ppermute | solution.py:331
  (19 other events, 135.0 us)
